TPU v7x, 256 devices: a whole 4x4x8 slice. The times are simulated.
256 devices in a mesh: space: 16 (over x_lo, z), snap: 16 (over x_hi, y, core).
Axes of the slice: x: 4 (x_hi: 2, x_lo: 2; x = x_hi * 2 + x_lo), y: 4, z: 8, core: 2. Of those that a mesh axis runs over, the one named last changes fastest.
Arguments:
- snapshots: bfloat16 [1048576, 512], P('space', 'snap'), may hold values from -6 to 6
- mass_blocks: bfloat16 [8192, 3, 128, 128], P(('space', 'snap')), may hold values from -0.3125 to 0.3125
- neighbours: int32 [8192, 3], P(('space', 'snap')), may hold values from 0 to 8191, as said below
- eigvecs: bfloat16 [512, 128], replicated, may hold values from -0.25 to 0.25
Outputs:
- weighted: bfloat16 [1048576, 512], P(('space', 'snap'))
- correlation: float32 [512, 512], P('snap', 'space')
- modes: bfloat16 [1048576, 128], P(('space', 'snap'))
Inputs may be any that keep to these rules, and one draw needn't show every extreme that they name: neighbours[b, 0] is b; every entry lies within 4 of b; neighbours[b, 2] lies exactly 4 away from b.
All inputs are finite; a program needn't handle non-finite values.
Results may differ from a plain program's by a relative error of at most 0.0029.
Values may be sent and summed in bfloat16 or wider, within the bound.
No kernel may reach another device: no remote copies, remote signals or barrier semaphores. Data moves between devices by JAX's collectives and lax.ppermute only.
A program may use at most 128 MiB of HBM per device.

v0:
```python
import jax
import jax.numpy as jnp
from jax import lax
from jax.sharding import PartitionSpec as P

HB = 4


def shifted(block, axis, distance):
    devices = range(lax.axis_size(axis))
    route = [(i - distance, i) for i in devices if i - distance in devices]
    return lax.ppermute(block, axis, route)


def shards(snapshots, mass_blocks, neighbours, eigvecs):
    local_rows = lax.all_to_all(snapshots, "snap", split_axis=0, concat_axis=1, tiled=True)
    row_count, col_count = local_rows.shape
    block_size = mass_blocks.shape[2]
    rim_rows = HB * block_size
    below_rim = shifted(local_rows[row_count - rim_rows :], ("space", "snap"), 1)
    above_rim = shifted(local_rows[:rim_rows], ("space", "snap"), -1)
    extended = jnp.concatenate([below_rim, local_rows, above_rim], axis=0).reshape(
        -1, block_size, col_count
    )
    first_block = lax.axis_index(("space", "snap")) * (row_count // block_size)
    local_ids = neighbours - first_block + HB
    nearby = extended[local_ids]
    weighted = jnp.einsum("bjrc,bjcs->brs", mass_blocks, nearby, preferred_element_type=jnp.float32)
    weighted = weighted.reshape(row_count, col_count).astype(jnp.bfloat16)
    partial_corr = jnp.dot(weighted.T, local_rows, preferred_element_type=jnp.float32)
    tile_rows = col_count // lax.axis_size("snap")
    tile_cols = col_count // lax.axis_size("space")
    summed = lax.psum(partial_corr, ("space", "snap"))
    row_start = lax.axis_index("snap") * tile_rows
    col_start = lax.axis_index("space") * tile_cols
    correlation = lax.dynamic_slice(summed, (row_start, col_start), (tile_rows, tile_cols))
    cell_total = row_count * lax.axis_size("space") * lax.axis_size("snap")
    correlation = correlation * (1.0 / cell_total)
    modes = jnp.dot(local_rows, eigvecs, preferred_element_type=jnp.float32).astype(jnp.bfloat16)
    return (weighted, correlation, modes)


def solution(mesh):
    in_specs = (
        P("space", "snap"),
        P(("space", "snap"), None, None, None),
        P(("space", "snap"), None),
        P(),
    )
    out_specs = (P(("space", "snap"), None), P("snap", "space"), P(("space", "snap"), None))
    return jax.shard_map(shards, mesh=mesh, in_specs=in_specs, out_specs=out_specs, check_vma=False)
```

profile of v0, /device:TPU:2, one launch (start us, length us, event | category | flops | bytes accessed | tf_op | source)
XLA Modules:
  0.0 392.4 jit_solution(7844460466667527686)
XLA Ops:
  7.2 0.0 copy-start
  7.2 0.0 all-reduce.2.cloned.1.call-start
  7.2 2.6 copy.21
  9.8 0.0 copy-start.5
  9.8 57.6 %all_to_all.19 = bf16[16,4096,32]{1,2,0:T(8,128)(2,1)S(1)} all-to-all(bf16[16,4096,32]{1,2,0:T(8,128)(2,1)S(1)} %bitcast.29), channel_id=1, replica_groups=mesh['space'=16,'snap'=16] {'snap'}, dimensions={0} | all-to-all | bytes 8388608 | tf_op jit(solution)/shard_map/all_to_all | solution.py:16
  67.5 2.0 copy-done.1
  69.5 1.1 fusion
  70.6 1.9 collective-permute-start
  72.5 7.9 %collective-permute-start.1 = (bf16[512,512]{0,1:T(8,128)(2,1)}, bf16[512,512]{0,1:T(8,128)(2,1)}, u32[]{:S(2)}, u32[]{:S(2)}) collective-permute-start(bf16[512,512]{0,1:T(8,128)(2,1)} %bitcast.3), channel_id=1, source_target_pairs={{1,0},{2,1},{3,2},{4,3},{5,4},{6,5},{7,6},{8,7},{9,8},{10,9},{11,1... | collective-permute-start | bytes 1572872 | tf_op jit(solution)/shard_map/ppermute | solution.py:12
  80.4 0.1 copy.17
  80.5 0.1 reshape.20
  80.6 5.0 %collective-permute-done = bf16[512,512]{0,1:T(8,128)(2,1)} collective-permute-done((bf16[512,512]{0,1:T(8,128)(2,1)}, bf16[512,512]{0,1:T(8,128)(2,1)}, u32[]{:S(2)}, u32[]{:S(2)}) %collective-permute-start) | collective-permute-done | bytes 524320 | tf_op jit(solution)/shard_map/ppermute | solution.py:12
  85.6 1.8 collective-permute-done.1
  87.4 5.7 %pad_maximum_fusion = bf16[5120,512]{0,1:T(8,128)(2,1)} fusion(bf16[512,512]{0,1:T(8,128)(2,1)} %collective-permute-done.1, bf16[4096,512]{0,1:T(8,128)(2,1)} %bitcast.26, bf16[512,512]{0,1:T(8,128)(2,1)} %collective-permute-done), kind=kLoop, calls=%fused_computation.2 | loop fusion | flops 15728640 | bytes 10485760 | tf_op jit(solution)/shard_map/concatenate | solution.py:22
  93.1 7.8 %copy.16 = bf16[5120,512]{1,0:T(8,128)(2,1)} copy(bf16[5120,512]{0,1:T(8,128)(2,1)} %pad_maximum_fusion) | data formatting | bytes 10485760 | tf_op jit(solution)/shard_map/concatenate | solution.py:22
  100.9 9.3 %gather_fusion = bf16[96,128,512]{2,1,0:T(8,128)(2,1)} fusion(bf16[40,128,512]{2,1,0:T(8,128)(2,1)} %bitcast.24, s32[1024]{0:T(1024)S(1)} %pad_clamp_fusion), kind=kCustom, calls=%fused_computation | custom fusion | bytes 25166208 | tf_op jit(solution)/shard_map/gather | solution.py:27
  110.3 7.1 %bitcast_convert_fusion = bf16[32,512,128]{1,2,0:T(8,128)(2,1)S(1)} fusion(bf16[32,3,128,128]{3,2,1,0:T(8,128)(2,1)S(1)} %copy-done, bf16[32,3,128,512]{3,2,1,0:T(8,128)(2,1)} %bitcast.23), kind=kOutput, calls=%fused_computation.1 | convolution fusion | flops 1612709888 | bytes 19922944 | tf_op jit(solution)/shard_map/bjrc,bjcs->brs/dot_general | solution.py:28
  117.3 0.0 copy-start.3
  117.3 2.0 copy-done.3
  119.4 3.4 fusion.1
  122.8 0.0 all-reduce.2.cloned.1.call-update
  122.8 4.5 %convolution_convert_fusion = bf16[4096,128]{1,0:T(8,128)(2,1)} fusion(bf16[4096,512]{0,1:T(8,128)(2,1)} %bitcast.27, bf16[512,128]{1,0:T(8,128)(2,1)S(1)} %copy-done.4), kind=kOutput, calls=%fused_computation.3 | convolution fusion | flops 537395200 | bytes 5373952 | tf_op jit(solution)/shard_map/dot_general | solution.py:39
  127.3 256.9 %all-reduce.2.cloned.1.call-done = f32[512,512]{1,0:T(8,128)} async-done(((f32[512,512]{1,0:T(8,128)}), f32[512,512]{1,0:T(8,128)}) %all-reduce.2.cloned.1.call-update) | async-done | bytes 1048592 | tf_op jit(solution)/shard_map/psum | solution.py:33
  384.2 1.4 dynamic-slice_multiply_fusion
  (9 shorter events, 0.0 us)
Async XLA Ops:
  7.2 103.1 %copy-start = (bf16[32,3,128,128]{3,2,1,0:T(8,128)(2,1)S(1)}, bf16[32,3,128,128]{3,2,1,0:T(8,128)(2,1)}, u32[]{:S(2)}) copy-start(bf16[32,3,128,128]{3,2,1,0:T(8,128)(2,1)} %param.5) | copy-start | bytes 9437188
  7.2 377.0 %all-reduce.2.cloned.1.call-start = ((), (), s32[]{:S(2)}) async-start(), calls=%async_computation.1 | async-start | bytes 2097152 | tf_op jit(solution)/shard_map/psum | solution.py:33
  9.8 70.5 %copy-start.5 = (s32[32,3]{0,1:T(4,128)S(1)}, s32[32,3]{0,1:T(4,128)}, u32[]{:S(2)}) copy-start(s32[32,3]{0,1:T(4,128)} %param.6) | copy-start | bytes 1156
  67.5 2.0 copy-start.1
  70.6 15.0 %collective-permute-start = (bf16[512,512]{0,1:T(8,128)(2,1)}, bf16[512,512]{0,1:T(8,128)(2,1)}, u32[]{:S(2)}, u32[]{:S(2)}) collective-permute-start(bf16[512,512]{0,1:T(8,128)(2,1)} %bitcast.1), channel_id=1, source_target_pairs={{0,1},{1,2},{2,3},{3,4},{4,5},{5,6},{6,7},{7,8},{8,9},{9,10},{10,1... | collective-permute-start | bytes 1572872 | tf_op jit(solution)/shard_map/ppermute | solution.py:12
  72.5 14.9 %collective-permute-start.1 = (bf16[512,512]{0,1:T(8,128)(2,1)}, bf16[512,512]{0,1:T(8,128)(2,1)}, u32[]{:S(2)}, u32[]{:S(2)}) collective-permute-start(bf16[512,512]{0,1:T(8,128)(2,1)} %bitcast.3), channel_id=1, source_target_pairs={{1,0},{2,1},{3,2},{4,3},{5,4},{6,5},{7,6},{8,7},{9,8},{10,9},{11,1... | collective-permute-start | bytes 1572872 | tf_op jit(solution)/shard_map/ppermute | solution.py:12
  110.3 9.1 %copy-start.2 = (bf16[16,4096,32]{1,2,0:T(8,128)(2,1)S(1)}, bf16[16,4096,32]{1,2,0:T(8,128)(2,1)}, u32[]{:S(2)}) copy-start(bf16[16,4096,32]{1,2,0:T(8,128)(2,1)} %copy-done.1) | copy-start | bytes 12582916
  117.3 2.0 copy-start.3
  119.4 3.4 copy-start.4
Sparse Core Ops, SparseCore 0:
  122.9 261.2 all-reduce.1
where the time goes:
time: 393 us; the launch traced here: 392 us
  waiting for transfers between devices  264 us (67%)
  blocking collectives  57.6 us (15%)
  local copies, waits for them, and re-layouts  25.1 us (6%)
  matrix products  14.9 us (4%)
  between operations  14.1 us (4%)
  starting transfers between devices  9.81 us (2%)
  other arithmetic  7.16 us (2%)
    psum x1, waiting for transfers between devices, shards(): summed = lax.psum(partial_corr, ('space', 'snap'))  257 us
    all_to_all x1, blocking collectives, shards(): lax.all_to_all(snapshots, 'snap', split_axis=0, concat_axis=1, tiled=True)  57.6 us
    ppermute x2, starting transfers between devices, shifted(): return lax.ppermute(block, axis, route)  9.77 us
    gather x1, local copies, waits for them, and re-layouts, shards(): nearby = extended[local_ids]  9.32 us
  transfers between devices with their start and end apart: 3, of which 3 were waited for; matrix products, arithmetic and copies ran while one was open for 1% of the time, Pallas kernels for 0%

commit v1 on v0

v1 whole, which is shorter than its diff:
```python
import jax
import jax.numpy as jnp
from jax import lax
from jax.experimental import pallas as pl
from jax.experimental.pallas import tpu as pltpu
from jax.sharding import PartitionSpec as P

HB = 4
STEP = 4
AXES = ("space", "snap")
MIB = 1 << 20


def contract(a, b, dim_a, dim_b):
    return lax.dot_general(a, b, (((dim_a,), (dim_b,)), ((), ())), preferred_element_type=jnp.float32)


def weigh(place, blocks, mass_ref, field_ref, weighted_ref, size):
    for k in range(blocks):
        near = [field_ref[:, pl.ds(pl.multiple_of(place(k, j) * size, size), size)] for j in range(3)]
        mass = [mass_ref[k, j] for j in range(3)]
        block = contract(jnp.concatenate(mass, axis=1), jnp.concatenate(near, axis=1), 1, 1)
        weighted_ref[k * size : (k + 1) * size, :] = block.astype(weighted_ref.dtype)


def interior_kernel(where_ref, neighbours_ref, field_ref, mass_ref, weighted_ref, corr_ref):
    step = pl.program_id(0)
    size = mass_ref.shape[2]

    def place(k, j):
        return neighbours_ref[j, (step + 1) * STEP + k] - where_ref[0]

    @pl.when(step == 0)
    def _():
        corr_ref[...] = jnp.zeros_like(corr_ref)

    weigh(place, STEP, mass_ref, field_ref, weighted_ref, size)
    width = STEP * size
    own = field_ref[:, pl.ds(pl.multiple_of((step + 1) * width, width), width)]
    corr_ref[...] += contract(own, weighted_ref[...], 1, 0)


def rim_kernel(where_ref, neighbours_ref, field_ref, below_ref, above_ref, mass_ref, corr_in_ref, _, weighted_ref,
               keep_ref, send_ref, extended, corr):
    step = pl.program_id(0)
    size = mass_ref.shape[2]
    width = STEP * size
    count = neighbours_ref.shape[1]
    first = step * (count - STEP)

    def place(k, j):
        return neighbours_ref[j, first + k] - where_ref[0] - first + HB

    @pl.when(step == 0)
    def _():
        corr[...] = corr_in_ref[...]
        extended[:, :width] = below_ref[...]
        extended[:, width:] = field_ref[...]

    @pl.when(step == 1)
    def _():
        extended[:, : 2 * width] = field_ref[...]
        extended[:, 2 * width :] = above_ref[...]

    weigh(place, STEP, mass_ref, extended, weighted_ref, size)
    corr[...] += contract(extended[:, width : 2 * width], weighted_ref[...], 1, 0)

    @pl.when(step == 1)
    def _():
        corr[...] = corr[...].T
        core = where_ref[1]
        tile = keep_ref.shape[1]
        for k in range(keep_ref.shape[0]):
            keep_ref[k] = corr[pl.ds(pl.multiple_of((2 * k + core) * tile, tile), tile), :]
            send_ref[k] = corr[pl.ds(pl.multiple_of((2 * k + 1 - core) * tile, tile), tile), :]


def modes_kernel(field_ref, vectors_ref, modes_ref):
    modes_ref[...] = contract(vectors_ref[...], field_ref[...], 0, 0).T.astype(modes_ref.dtype)


def flipped(value, mask):
    return lax.ppermute(value, AXES, [(i, i ^ mask) for i in range(lax.axis_size(AXES))])


def shifted(value, distance):
    count = lax.axis_size(AXES)
    return lax.ppermute(value, AXES, [(i, (i + distance) % count) for i in range(count)])


def shards(snapshots, mass_blocks, neighbours, eigvecs):
    cells, mine = snapshots.shape
    group = lax.axis_size("snap")
    spaces = lax.axis_size("space")
    rows = cells // group
    snaps = mine * group
    count, _, size, _ = mass_blocks.shape
    width = STEP * size
    modes_count = eigvecs.shape[1]

    parts = snapshots.T.reshape(mine, group, rows).transpose(1, 0, 2)
    field = lax.all_to_all(parts, "snap", split_axis=0, concat_axis=0).reshape(snaps, rows)
    below = shifted(field[:, rows - width :], 1)
    above = shifted(field[:, :width], -1)

    where = jnp.stack([lax.axis_index(AXES) * count, lax.axis_index("snap") & 1]).astype(jnp.int32)
    listed = neighbours.T
    scalar = pl.BlockSpec(memory_space=pltpu.SMEM)
    inner = count // STEP - 2
    weighted, corr = pl.pallas_call(
        interior_kernel,
        grid=(inner,),
        in_specs=[
            scalar,
            scalar,
            pl.BlockSpec((snaps, rows), lambda i: (0, 0)),
            pl.BlockSpec((STEP, 3, size, size), lambda i: (i + 1, 0, 0, 0)),
        ],
        out_specs=[
            pl.BlockSpec((width, snaps), lambda i: (i + 1, 0)),
            pl.BlockSpec((snaps, snaps), lambda i: (0, 0)),
        ],
        out_shape=[
            jax.ShapeDtypeStruct((rows, snaps), jnp.bfloat16),
            jax.ShapeDtypeStruct((snaps, snaps), jnp.float32),
        ],
        compiler_params=pltpu.CompilerParams(vmem_limit_bytes=28 * MIB),
        cost_estimate=pl.CostEstimate(flops=inner * 2 * width * snaps * (3 * size + snaps), bytes_accessed=12 * MIB, transcendentals=0),
        name="interior",
    )(where, listed, field, mass_blocks)

    last = rows // (2 * width) - 1
    weighted, keep, send = pl.pallas_call(
        rim_kernel,
        grid=(2,),
        in_specs=[
            scalar,
            scalar,
            pl.BlockSpec((snaps, 2 * width), lambda i: (0, i * last)),
            pl.BlockSpec((snaps, width), lambda i: (0, 0)),
            pl.BlockSpec((snaps, width), lambda i: (0, 0)),
            pl.BlockSpec((STEP, 3, size, size), lambda i: (i * (inner + 1), 0, 0, 0)),
            pl.BlockSpec((snaps, snaps), lambda i: (0, 0)),
            pl.BlockSpec(memory_space=pl.ANY),
        ],
        out_specs=[
            pl.BlockSpec((width, snaps), lambda i: (i * (inner + 1), 0)),
            pl.BlockSpec((group // 2, mine, snaps), lambda i: (0, 0, 0)),
            pl.BlockSpec((group // 2, mine, snaps), lambda i: (0, 0, 0)),
        ],
        out_shape=[
            jax.ShapeDtypeStruct((rows, snaps), jnp.bfloat16),
            jax.ShapeDtypeStruct((group // 2, mine, snaps), jnp.float32),
            jax.ShapeDtypeStruct((group // 2, mine, snaps), jnp.float32),
        ],
        scratch_shapes=[pltpu.VMEM((snaps, 3 * width), jnp.bfloat16), pltpu.VMEM((snaps, snaps), jnp.float32)],
        input_output_aliases={7: 0},
        compiler_params=pltpu.CompilerParams(vmem_limit_bytes=28 * MIB),
        cost_estimate=pl.CostEstimate(flops=4 * width * snaps * (3 * size + snaps), bytes_accessed=8 * MIB, transcendentals=0),
        name="rim",
    )(where, listed, field, below, above, mass_blocks, corr, weighted)

    summed = keep + flipped(send, 1)
    chips = [[2 * k + core for k in range(group // 2)] for core in range(2)]
    summed = lax.all_to_all(summed, "snap", split_axis=0, concat_axis=0, axis_index_groups=chips).sum(0)
    tiles = summed.reshape(mine, spaces, snaps // spaces).transpose(1, 0, 2)
    correlation = lax.all_to_all(tiles, "space", split_axis=0, concat_axis=0).sum(0)
    correlation = correlation * (1.0 / (rows * lax.axis_size(AXES)))

    modes = pl.pallas_call(
        modes_kernel,
        grid=(rows // 1024,),
        in_specs=[
            pl.BlockSpec((snaps, 1024), lambda i: (0, i)),
            pl.BlockSpec((snaps, modes_count), lambda i: (0, 0)),
        ],
        out_specs=pl.BlockSpec((1024, modes_count), lambda i: (i, 0)),
        out_shape=jax.ShapeDtypeStruct((rows, modes_count), jnp.bfloat16),
        compiler_params=pltpu.CompilerParams(vmem_limit_bytes=16 * MIB),
        cost_estimate=pl.CostEstimate(flops=2 * rows * snaps * modes_count, bytes_accessed=5 * MIB, transcendentals=0),
        name="modes",
    )(field, eigvecs)
    return weighted, correlation, modes


def solution(mesh):
    in_specs = (
        P("space", "snap"),
        P(AXES, None, None, None),
        P(AXES, None),
        P(),
    )
    out_specs = (P(AXES, None), P("snap", "space"), P(AXES, None))
    return jax.shard_map(shards, mesh=mesh, in_specs=in_specs, out_specs=out_specs, check_vma=False)
```

time: 393 us -> 124 us (0.32)
  waiting for transfers between devices: 264 us -> 4.12 us
  blocking collectives: 57.6 us -> 75.6 us
  matrix products: 14.9 us -> 0 us
  Pallas kernels: 0 us -> 14.9 us
  local copies, waits for them, and re-layouts: 25.1 us -> 11.5 us
  between operations: 14.1 us -> 0.71 us
  starting transfers between devices: 9.81 us -> 15.8 us
  other arithmetic: 7.16 us -> 1.63 us
    psum x1 -> x0, waiting for transfers between devices: 257 us -> none  [shards(): summed = lax.psum(partial_corr, ('space', 'snap'))]
    all_to_all x1 -> x2, blocking collectives: 57.6 us -> 75.6 us  [the longest x1 57.9 us: shards(): lax.all_to_all(parts, 'snap', split_axis=0, concat_axis=0)]
    dot_general x3 -> x0, matrix products: 14.9 us -> none  [the longest x1 7.06 us: shards(): jnp.einsum('bjrc,bjcs->brs', mass_blocks, nearby, preferred_element_type=...]
    pallas_call x0 -> x3, Pallas kernels: none -> 14.9 us  [the longest x1 7.31 us: shards(): pl.pallas_call(interior_kernel, grid=(inner,), in_specs=[scalar, scalar,...]
    all_to_all x0 -> x1, starting transfers between devices: none -> 9.81 us  [shards(): lax.all_to_all(tiles, 'space', split_axis=0, concat_axis=0).sum(0)]
    gather x1 -> x0, local copies, waits for them, and re-layouts: 9.32 us -> none  [shards(): nearby = extended[local_ids]]
    concatenate x1 -> x0, local copies, waits for them, and re-layouts: 7.83 us -> none  [shards(): jnp.concatenate([below_rim, local_rows, above_rim], axis=0)]
    concatenate x1 -> x0, other arithmetic: 5.75 us -> none  [shards(): jnp.concatenate([below_rim, local_rows, above_rim], axis=0)]
  transfers between devices with their start and end apart: 3 -> 4, of which waited for: 3 -> 2; matrix products, arithmetic and copies ran while one was open for 1% -> 0% of each run, Pallas kernels for 0% -> 8%
where the time goes in v1:
time: 124 us
  blocking collectives  75.6 us (61%)
  starting transfers between devices  15.8 us (13%)
  Pallas kernels  14.9 us (12%)
  local copies, waits for them, and re-layouts  11.5 us (9%)
  waiting for transfers between devices  4.12 us (3%)
  other arithmetic  1.63 us (1%)
    all_to_all x1, blocking collectives, shards(): lax.all_to_all(parts, 'snap', split_axis=0, concat_axis=0)  57.9 us
    all_to_all x1, blocking collectives, shards(): lax.all_to_all(summed, 'snap', split_axis=0, concat_axis=0, axis_index_gr...  17.7 us
    all_to_all x1, starting transfers between devices, shards(): lax.all_to_all(tiles, 'space', split_axis=0, concat_axis=0).sum(0)  9.81 us
    pallas_call x1, Pallas kernels, shards(): pl.pallas_call(interior_kernel, grid=(inner,), in_specs=[scalar, scalar,...  7.31 us
    unnamed x14, local copies, waits for them, and re-layouts  7.21 us
    ppermute x2, starting transfers between devices, shifted(): lax.ppermute(value, AXES, [(i, (i + distance) % count) for i in range(cou...  5.96 us
    pallas_call x1, Pallas kernels, shards(): pl.pallas_call(rim_kernel, grid=(2,), in_specs=[scalar, scalar, pl.BlockS...  4.7 us
    pallas_call x1, Pallas kernels, shards(): pl.pallas_call(modes_kernel, grid=(rows // 1024,), in_specs=[pl.BlockSpec...  2.85 us
  transfers between devices with their start and end apart: 4, of which 2 were waited for; matrix products, arithmetic and copies ran while one was open for 0% of the time, Pallas kernels for 8%

profile of v1, /device:TPU:2, one launch (start us, length us, event | category | flops | bytes accessed | tf_op | source)
XLA Modules:
  0.0 124.1 jit_solution(16502012725999575894)
XLA Ops:
  0.6 2.5 %copy.14 = bf16[4,16,8,4096]{3,2,0,1:T(8,128)(2,1)S(1)} copy(bf16[4,16,8,4096]{3,2,1,0:T(8,128)(2,1)} %bitcast.20) | data formatting | bytes 8388608 | tf_op jit(solution)/shard_map/reshape | solution.py:101
  3.1 0.0 copy-start.3
  3.1 57.9 %all_to_all.15 = bf16[16,32,4096]{2,1,0:T(8,128)(2,1)S(1)} all-to-all(bf16[16,32,4096]{2,1,0:T(8,128)(2,1)S(1)} %bitcast.19), channel_id=1, replica_groups=mesh['space'=16,'snap'=16] {'snap'}, dimensions={0} | all-to-all | bytes 8388608 | tf_op jit(solution)/shard_map/all_to_all | solution.py:102
  61.0 1.1 fusion
  62.1 1.9 %copy-done = bf16[16,32,4096]{2,1,0:T(8,128)(2,1)} copy-done((bf16[16,32,4096]{2,1,0:T(8,128)(2,1)}, bf16[16,32,4096]{2,1,0:T(8,128)(2,1)S(1)}, u32[]{:S(2)}) %copy-start) | copy-done | bytes 4194328
  64.0 6.0 %collective-permute-start.1 = (bf16[512,512]{1,0:T(8,128)(2,1)}, bf16[512,512]{1,0:T(8,128)(2,1)}, u32[]{:S(2)}, u32[]{:S(2)}) collective-permute-start(bf16[512,512]{1,0:T(8,128)(2,1)} %get-tuple-element.13), channel_id=1, source_target_pairs={{0,255},{1,0},{2,1},{3,2},{4,3},{5,4},{6,5},{7,6},{8,7},{9,8},{10,... | collective-permute-start | bytes 1572872 | tf_op jit(solution)/shard_map/ppermute | solution.py:88
  70.0 0.1 pad_add_fusion.where_ref
  70.1 2.2 %copy-done.1 = bf16[16,32,4096]{2,1,0:T(8,128)(2,1)S(1)} copy-done((bf16[16,32,4096]{2,1,0:T(8,128)(2,1)S(1)}, bf16[16,32,4096]{2,1,0:T(8,128)(2,1)}, u32[]{:S(2)}) %copy-start.1) | copy-done | bytes 4194328
  72.3 7.3 %interior.1 = (bf16[4096,512]{1,0:T(8,128)(2,1)}, f32[512,512]{1,0:T(8,128)S(1)}) custom-call(s32[2]{0:T(128)S(1)} %pad_add_fusion.where_ref, s32[3,32]{1,0:T(4,128)S(1)} %bitcast.17, bf16[512,4096]{1,0:T(8,128)(2,1)S(1)} %bitcast.14, bf16[32,3,128,128]{3,2,1,0:T(8,128)(2,1)S(1)} %copy-done.3), custom_call_target="tpu_custom_call" | custom-call | flops 2818572288 | bytes 12582912 | tf_op jit(solution)/shard_map/interior/pallas_call | solution.py:110
  79.6 4.7 %rim.1 = (bf16[4096,512]{1,0:T(8,128)(2,1)}, f32[8,32,512]{2,1,0:T(8,128)S(1)}, f32[8,32,512]{2,1,0:T(8,128)S(1)}) custom-call(s32[2]{0:T(128)S(1)} %pad_add_fusion.where_ref, s32[3,32]{1,0:T(4,128)S(1)} %bitcast.18, bf16[512,4096]{1,0:T(8,128)(2,1)S(1)} %bitcast.15, ...), custom_call_target="tpu_custom_call", output_to_operand_aliasing={{0}: (7, {})} | custom-call | flops 939524096 | bytes 8388608 | tf_op jit(solution)/shard_map/rim/pallas_call | solution.py:133
  84.3 1.9 %collective-permute-done.2 = f32[8,32,512]{2,1,0:T(8,128)S(1)} collective-permute-done((f32[8,32,512]{2,1,0:T(8,128)S(1)}, f32[8,32,512]{2,1,0:T(8,128)S(1)}, u32[]{:S(2)}, u32[]{:S(2)}) %collective-permute-start.2) | collective-permute-done | bytes 524320 | tf_op jit(solution)/shard_map/ppermute | solution.py:83
  86.2 0.1 add.7
  86.3 17.7 %all_to_all.16 = f32[8,32,512]{2,1,0:T(8,128)S(1)} all-to-all(f32[8,32,512]{2,1,0:T(8,128)S(1)} %add.7), channel_id=1, replica_groups={{0,2,4,6,8,10,12,14},{1,3,5,7,9,11,13,15},{16,18,20,22,24,26,28,30},{17..., dimensions={0} | all-to-all | bytes 1048576 | tf_op jit(solution)/shard_map/all_to_all | solution.py:165
  104.0 0.1 reshape.17
  104.1 0.1 copy.11
  104.2 0.8 reshape.18
  105.0 9.8 %all-to-all-start.2 = ((f32[16,1,1024]{2,1,0:T(1,128)}), f32[16,1,1024]{2,1,0:T(1,128)S(1)}, u32[]{:S(2)}, u32[]{:S(2)}) async-start(f32[16,1,1024]{2,1,0:T(1,128)} %reshape.18), calls=%async_computation.2 | async-start | bytes 131072 | tf_op jit(solution)/shard_map/all_to_all | solution.py:167
  114.8 2.2 %copy-done.2 = bf16[16,32,4096]{2,1,0:T(8,128)(2,1)S(1)} copy-done((bf16[16,32,4096]{2,1,0:T(8,128)(2,1)S(1)}, bf16[16,32,4096]{2,1,0:T(8,128)(2,1)}, u32[]{:S(2)}) %copy-start.2) | copy-done | bytes 4194328
  117.0 2.8 %modes.1 = bf16[4096,128]{1,0:T(8,128)(2,1)} custom-call(bf16[512,4096]{1,0:T(8,128)(2,1)S(1)} %bitcast.16, bf16[512,128]{1,0:T(8,128)(2,1)S(1)} %copy-done.4), custom_call_target="tpu_custom_call" | custom-call | flops 536870912 | bytes 5242880 | tf_op jit(solution)/shard_map/modes/pallas_call | solution.py:170
  119.8 2.2 %all-to-all-done.2 = f32[16,1,1024]{2,1,0:T(1,128)S(1)} async-done(((f32[16,1,1024]{2,1,0:T(1,128)}), f32[16,1,1024]{2,1,0:T(1,128)S(1)}, u32[]{:S(2)}, u32[]{:S(2)}) %all-to-all-start.2) | async-done | bytes 65568 | tf_op jit(solution)/shard_map/all_to_all | solution.py:167
  122.0 0.5 broadcast
  122.5 0.8 reduce
  123.4 0.1 reshape.19
  123.5 0.6 broadcast_multiply_fusion
  (14 shorter events, 0.1 us)
Async XLA Ops:
  3.1 67.0 %copy-start.3 = (bf16[32,3,128,128]{3,2,1,0:T(8,128)(2,1)S(1)}, bf16[32,3,128,128]{3,2,1,0:T(8,128)(2,1)}, u32[]{:S(2)}) copy-start(bf16[32,3,128,128]{3,2,1,0:T(8,128)(2,1)} %mass_ref.3) | copy-start | bytes 9437188
  3.1 67.0 %copy-start.5 = (s32[32,3]{0,1:T(4,128)S(1)}, s32[32,3]{0,1:T(4,128)}, u32[]{:S(2)}) copy-start(s32[32,3]{0,1:T(4,128)} %param.6) | copy-start | bytes 1156
  62.1 1.9 %copy-start = (bf16[16,32,4096]{2,1,0:T(8,128)(2,1)}, bf16[16,32,4096]{2,1,0:T(8,128)(2,1)S(1)}, u32[]{:S(2)}) copy-start(bf16[16,32,4096]{2,1,0:T(8,128)(2,1)S(1)} %all_to_all.15) | copy-start | bytes 12582916
  64.0 15.5 %collective-permute-start = (bf16[512,512]{1,0:T(8,128)(2,1)}, bf16[512,512]{1,0:T(8,128)(2,1)}, u32[]{:S(2)}, u32[]{:S(2)}) collective-permute-start(bf16[512,512]{1,0:T(8,128)(2,1)} %get-tuple-element.14), channel_id=1, source_target_pairs={{0,1},{1,2},{2,3},{3,4},{4,5},{5,6},{6,7},{7,8},{8,9},{9,10},{10,1... | collective-permute-start | bytes 1572872 | tf_op jit(solution)/shard_map/ppermute | solution.py:88
  64.0 15.5 %collective-permute-start.1 = (bf16[512,512]{1,0:T(8,128)(2,1)}, bf16[512,512]{1,0:T(8,128)(2,1)}, u32[]{:S(2)}, u32[]{:S(2)}) collective-permute-start(bf16[512,512]{1,0:T(8,128)(2,1)} %get-tuple-element.13), channel_id=1, source_target_pairs={{0,255},{1,0},{2,1},{3,2},{4,3},{5,4},{6,5},{7,6},{8,7},{9,8},{10,... | collective-permute-start | bytes 1572872 | tf_op jit(solution)/shard_map/ppermute | solution.py:88
  70.1 2.2 %copy-start.1 = (bf16[16,32,4096]{2,1,0:T(8,128)(2,1)S(1)}, bf16[16,32,4096]{2,1,0:T(8,128)(2,1)}, u32[]{:S(2)}) copy-start(bf16[16,32,4096]{2,1,0:T(8,128)(2,1)} %copy-done) | copy-start | bytes 12582916
  84.3 30.5 %copy-start.4 = (bf16[512,128]{1,0:T(8,128)(2,1)S(1)}, bf16[512,128]{1,0:T(8,128)(2,1)}, u32[]{:S(2)}) copy-start(bf16[512,128]{1,0:T(8,128)(2,1)} %vectors_ref.1) | copy-start | bytes 393220
  84.3 1.9 %collective-permute-start.2 = (f32[8,32,512]{2,1,0:T(8,128)S(1)}, f32[8,32,512]{2,1,0:T(8,128)S(1)}, u32[]{:S(2)}, u32[]{:S(2)}) collective-permute-start(f32[8,32,512]{2,1,0:T(8,128)S(1)} %get-tuple-element.12), channel_id=1, source_target_pairs={{0,1},{1,0},{2,3},{3,2},{4,5},{5,4},{6,7},{7,6},{8,9},{9,8},{10,11... | collective-permute-start | bytes 1572872 | tf_op jit(solution)/shard_map/ppermute | solution.py:83
  105.0 17.1 %all-to-all-start.2 = ((f32[16,1,1024]{2,1,0:T(1,128)}), f32[16,1,1024]{2,1,0:T(1,128)S(1)}, u32[]{:S(2)}, u32[]{:S(2)}) async-start(f32[16,1,1024]{2,1,0:T(1,128)} %reshape.18), calls=%async_computation.2 | async-start | bytes 131072 | tf_op jit(solution)/shard_map/all_to_all | solution.py:167
  114.8 2.2 %copy-start.2 = (bf16[16,32,4096]{2,1,0:T(8,128)(2,1)S(1)}, bf16[16,32,4096]{2,1,0:T(8,128)(2,1)}, u32[]{:S(2)}) copy-start(bf16[16,32,4096]{2,1,0:T(8,128)(2,1)} %copy-done) | copy-start | bytes 12582916

commit v2 on v0

v2 whole, which is shorter than its diff:
```python
import functools

import jax
import jax.numpy as jnp
from jax import lax
from jax.experimental import pallas as pl
from jax.experimental.pallas import tpu as pltpu
from jax.sharding import PartitionSpec as P

HB = 4
STEP = 4
AXES = ("space", "snap")
MIB = 1 << 20


def contract(a, b, dim_a, dim_b):
    return lax.dot_general(a, b, (((dim_a,), (dim_b,)), ((), ())), preferred_element_type=jnp.float32)


def weigh(place, blocks, mass_ref, field_ref, weighted_ref, size):
    for k in range(blocks):
        near = [field_ref[:, pl.ds(pl.multiple_of(place(k, j) * size, size), size)] for j in range(3)]
        mass = [mass_ref[k, j] for j in range(3)]
        block = contract(jnp.concatenate(mass, axis=1), jnp.concatenate(near, axis=1), 1, 1)
        weighted_ref[k * size : (k + 1) * size, :] = block.astype(weighted_ref.dtype)


def here():
    snap = lax.axis_index("snap")
    return lax.axis_index("space") * lax.axis_size("snap") + snap, lax.rem(snap, 2)


def chunks_kernel(field_ref, parts_ref, sems):
    group, _, length = parts_ref.shape
    own = field_ref.shape[1] // group
    halo = length - own
    copies = []
    for k in range(group):
        start, to, size = k * own - (1 - k % 2) * halo, 0, length
        if k == 0:
            start, to, size = 0, halo, own
        if k == group - 1:
            size = own
        source = field_ref.at[:, pl.ds(start, size)]
        copies.append(pltpu.make_async_copy(source, parts_ref.at[k, :, pl.ds(to, size)], sems.at[k]))
        copies[-1].start()
    for copy in copies:
        copy.wait()


def ends_kernel(before_ref, after_ref, parts_in_ref, parts_ref, sems):
    del parts_in_ref
    group, _, length = parts_ref.shape
    halo = before_ref.shape[1]
    copies = [
        pltpu.make_async_copy(before_ref, parts_ref.at[0, :, pl.ds(0, halo)], sems.at[0]),
        pltpu.make_async_copy(after_ref, parts_ref.at[group - 1, :, pl.ds(length - halo, halo)], sems.at[1]),
    ]
    for copy in copies:
        copy.start()
    for copy in copies:
        copy.wait()


def inner_kernel(neighbours_ref, field_ref, mass_ref, weighted_ref, corr_ref, copy_ref, edge_ref, next_ref, block,
                 block_sems, copy_sem):
    count, _, size, _ = mass_ref.shape
    width = STEP * size
    groups = count // STEP
    device, core = here()
    shift = device * count - (1 - core) * STEP
    own = pl.ds(pl.multiple_of((1 - core) * width, width), count * size)
    copy = pltpu.make_async_copy(field_ref.at[:, own], copy_ref, copy_sem)
    copy.start()
    edge_ref[...] = field_ref[:, pl.ds(pl.multiple_of((1 - core) * groups * width, width), width)]
    next_ref[...] = field_ref[:, pl.ds(pl.multiple_of(core * width + (1 - core) * (groups - 1) * width, width), width)]
    writes = []
    for step in range(groups - 1):
        slot = step % 2
        if len(writes) >= 2:
            writes[-2].wait()
        first = (step + core) * STEP

        def place(k, j):
            return neighbours_ref[j, first + k] - shift

        weigh(place, STEP, mass_ref.at[pl.ds(first, STEP)], field_ref, block.at[slot], size)
        rows = pl.ds(pl.multiple_of(first * size, width), width)
        writes.append(pltpu.make_async_copy(block.at[slot], weighted_ref.at[rows], block_sems.at[slot]))
        writes[-1].start()
        term = contract(field_ref[:, (step + 1) * width : (step + 2) * width], block[slot], 1, 0)
        corr_ref[...] = term if step == 0 else corr_ref[...] + term
    writes[-2].wait()
    writes[-1].wait()
    copy.wait()


def edge_kernel(neighbours_ref, edge_ref, next_ref, near_ref, mass_ref, corr_in_ref, weighted_in_ref, weighted_ref,
                keep_ref, send_ref, extended, block, block_sem, corr):
    del weighted_in_ref
    count, _, size, _ = mass_ref.shape
    width = STEP * size
    device, core = here()
    first = (1 - core) * (count - STEP)
    extended[:, width : 2 * width] = edge_ref[...]

    @pl.when(core == 0)
    def _():
        extended[:, :width] = next_ref[...]
        extended[:, 2 * width :] = near_ref[...]

    @pl.when(core != 0)
    def _():
        extended[:, :width] = near_ref[...]
        extended[:, 2 * width :] = next_ref[...]

    def place(k, j):
        return neighbours_ref[j, first + k] - device * count - first + HB

    weigh(place, STEP, mass_ref.at[pl.ds(first, STEP)], extended, block, size)
    rows = pl.ds(pl.multiple_of(first * size, width), width)
    write = pltpu.make_async_copy(block, weighted_ref.at[rows], block_sem)
    write.start()
    corr[...] = (corr_in_ref[...] + contract(edge_ref[...], block[...], 1, 0)).T
    tile = keep_ref.shape[1]
    for k in range(keep_ref.shape[0]):
        keep_ref[k] = corr[pl.ds(pl.multiple_of((2 * k + core) * tile, tile), tile), :]
        send_ref[k] = corr[pl.ds(pl.multiple_of((2 * k + 1 - core) * tile, tile), tile), :]
    write.wait()


def pack_kernel(parts_ref, packed_ref):
    total = parts_ref[0]
    for k in range(1, parts_ref.shape[0]):
        total = total + parts_ref[k]
    high, lanes = packed_ref.shape[1:]
    tile = total.shape[0]
    share = lanes // tile
    group = lax.broadcasted_iota(jnp.int32, (high, lanes), 1) // tile
    for k in range(packed_ref.shape[0]):
        piece = total[:, k // share * lanes : (k // share + 1) * lanes]
        packed = jnp.zeros((high, lanes), jnp.float32)
        for g in range(share):
            moved = piece[g * high : (g + 1) * high]
            turn = (g - k % share) % share * tile
            if turn:
                moved = pltpu.roll(moved, turn, 1)
            packed = jnp.where(group == g, moved, packed)
        packed_ref[k] = packed


def unpack_kernel(scale, packed_ref, tile_ref):
    total = packed_ref[0]
    for k in range(1, packed_ref.shape[0]):
        total = total + packed_ref[k]
    total = total * scale
    high = packed_ref.shape[1]
    tile = tile_ref.shape[1]
    share = packed_ref.shape[2] // tile
    for g in range(share):
        tile_ref[g * high : (g + 1) * high, :] = total[:, g * tile : (g + 1) * tile]


def modes_kernel(field_ref, vectors_ref, modes_ref):
    modes_ref[...] = contract(vectors_ref[...], field_ref[...], 0, 0).T.astype(modes_ref.dtype)


def flipped(value, mask):
    return lax.ppermute(value, AXES, [(i, i ^ mask) for i in range(lax.axis_size(AXES))])


def shifted(value, axis, distance):
    count = lax.axis_size(axis)
    return lax.ppermute(value, axis, [(i, (i + distance) % count) for i in range(count)])


def call(kernel, name, operands, out_shape, moved, flops=0, apart=(), out_apart=(), scratch=(), limit=24, **more):
    vmem, smem, anywhere = (pl.BlockSpec(memory_space=m) for m in (pltpu.VMEM, pltpu.SMEM, pl.ANY))
    specs = [smem if x.dtype == jnp.int32 else anywhere if k in apart else vmem for k, x in enumerate(operands)]
    return pl.pallas_call(
        kernel,
        in_specs=specs,
        out_specs=[anywhere if k in out_apart else vmem for k in range(len(out_shape))],
        out_shape=out_shape,
        scratch_shapes=scratch,
        compiler_params=pltpu.CompilerParams(vmem_limit_bytes=limit * MIB),
        cost_estimate=pl.CostEstimate(flops=flops, bytes_accessed=moved, transcendentals=0),
        name=name,
        **more,
    )(*operands)


def shards(snapshots, mass_blocks, neighbours, eigvecs):
    cells, mine = snapshots.shape
    group = lax.axis_size("snap")
    spaces = lax.axis_size("space")
    rows = cells // group
    snaps = mine * group
    size = mass_blocks.shape[2]
    width = STEP * size
    modes_count = eigvecs.shape[1]

    def half(*dims):
        return jax.ShapeDtypeStruct(dims, jnp.bfloat16)

    def single(*dims):
        return jax.ShapeDtypeStruct(dims, jnp.float32)

    sems = pltpu.SemaphoreType.DMA
    flat = snapshots.T
    before = shifted(flat[:, cells - width :], "space", 1)
    after = shifted(flat[:, :width], "space", -1)
    chunked = [half(group, mine, rows + width)]
    (parts,) = call(
        chunks_kernel, "chunks", (flat,), chunked, 8 * MIB, apart=(0,), out_apart=(0,), scratch=[sems((group,))]
    )
    (parts,) = call(
        ends_kernel,
        "ends",
        (before, after, parts),
        chunked,
        MIB // 16,
        apart=(0, 1, 2),
        out_apart=(0,),
        scratch=[sems((2,))],
        input_output_aliases={2: 0},
    )
    field = lax.all_to_all(parts, "snap", split_axis=0, concat_axis=0).reshape(snaps, rows + width)
    listed = neighbours.T
    per_row = 2 * snaps * (3 * size + snaps)
    weighted, corr, field, edge, following = call(
        inner_kernel,
        "inner",
        (listed, field, mass_blocks),
        [half(rows, snaps), single(snaps, snaps), half(snaps, rows)] + [half(snaps, width)] * 2,
        14 * MIB,
        (rows - width) * per_row,
        out_apart=(0, 2),
        scratch=[pltpu.VMEM((2, width, snaps), jnp.bfloat16), sems((2,)), sems(())],
    )
    near = flipped(edge, 1)
    modes = pl.pallas_call(
        modes_kernel,
        grid=(rows // 1024,),
        in_specs=[
            pl.BlockSpec((snaps, 1024), lambda i: (0, i)),
            pl.BlockSpec((snaps, modes_count), lambda i: (0, 0)),
        ],
        out_specs=pl.BlockSpec((1024, modes_count), lambda i: (i, 0)),
        out_shape=half(rows, modes_count),
        compiler_params=pltpu.CompilerParams(vmem_limit_bytes=16 * MIB),
        cost_estimate=pl.CostEstimate(flops=2 * rows * snaps * modes_count, bytes_accessed=5 * MIB, transcendentals=0),
        name="modes",
    )(field, eigvecs)
    weighted, keep, send = call(
        edge_kernel,
        "edge",
        (listed, edge, following, near, mass_blocks, corr, weighted),
        [half(rows, snaps)] + [single(group // 2, mine, snaps)] * 2,
        6 * MIB,
        width * per_row,
        apart=(6,),
        out_apart=(0,),
        scratch=[
            pltpu.VMEM((snaps, 3 * width), jnp.bfloat16),
            pltpu.VMEM((width, snaps), jnp.bfloat16),
            sems(()),
            pltpu.VMEM((snaps, snaps), jnp.float32),
        ],
        input_output_aliases={6: 0},
    )

    summed = keep + flipped(send, 1)
    chips = [[2 * k + core for k in range(group // 2)] for core in range(2)]
    summed = lax.all_to_all(summed, "snap", split_axis=0, concat_axis=0, axis_index_groups=chips)
    tile = snaps // spaces
    (packed,) = call(pack_kernel, "pack", (summed,), [single(spaces, mine * tile // 128, 128)], MIB)
    packed = lax.all_to_all(packed, "space", split_axis=0, concat_axis=0)
    scale = 1.0 / (rows * lax.axis_size(AXES))
    (correlation,) = call(functools.partial(unpack_kernel, scale), "unpack", (packed,), [single(mine, tile)], MIB)
    return weighted, correlation, modes


def solution(mesh):
    in_specs = (
        P("space", "snap"),
        P(AXES, None, None, None),
        P(AXES, None),
        P(),
    )
    out_specs = (P(AXES, None), P("snap", "space"), P(AXES, None))
    return jax.shard_map(shards, mesh=mesh, in_specs=in_specs, out_specs=out_specs, check_vma=False)
```

time: 393 us -> 120 us (0.31)
  waiting for transfers between devices: 264 us -> 9.21 us
  blocking collectives: 57.6 us -> 78.3 us
  local copies, waits for them, and re-layouts: 25.1 us -> 5.17 us
  matrix products: 14.9 us -> 0 us
  Pallas kernels: 0 us -> 14.7 us
  between operations: 14.1 us -> 0.73 us
  other arithmetic: 7.16 us -> 0.08 us
    psum x1 -> x0, waiting for transfers between devices: 257 us -> none  [shards(): summed = lax.psum(partial_corr, ('space', 'snap'))]
    all_to_all x1 -> x2, blocking collectives: 57.6 us -> 78.3 us  [the longest x1 63.8 us: shards(): lax.all_to_all(parts, 'snap', split_axis=0, concat_axis=0)]
    dot_general x3 -> x0, matrix products: 14.9 us -> none  [the longest x1 7.06 us: shards(): jnp.einsum('bjrc,bjcs->brs', mass_blocks, nearby, preferred_element_type=...]
    pallas_call x0 -> x7, Pallas kernels: none -> 14.7 us  [the longest x6 11.8 us: call(): pl.pallas_call(kernel, in_specs=specs, out_specs=[anywhere if k in out_ap...]
    gather x1 -> x0, local copies, waits for them, and re-layouts: 9.32 us -> none  [shards(): nearby = extended[local_ids]]
    concatenate x1 -> x0, local copies, waits for them, and re-layouts: 7.83 us -> none  [shards(): jnp.concatenate([below_rim, local_rows, above_rim], axis=0)]
    concatenate x1 -> x0, other arithmetic: 5.75 us -> none  [shards(): jnp.concatenate([below_rim, local_rows, above_rim], axis=0)]
    all_to_all x0 -> x1, starting transfers between devices: none -> 5.12 us  [shards(): packed = lax.all_to_all(packed, 'space', split_axis=0, concat_axis=0)]
  transfers between devices with their start and end apart: 3 -> 5, of which waited for: 3 -> 4; matrix products, arithmetic and copies ran while one was open for 1% -> 0% of each run, Pallas kernels for 0% -> 3%
where the time goes in v2:
time: 120 us; the launch traced here: 119 us
  blocking collectives  78.3 us (65%)
  Pallas kernels  14.7 us (12%)
  starting transfers between devices  11.3 us (9%)
  waiting for transfers between devices  9.21 us (8%)
  local copies, waits for them, and re-layouts  5.17 us (4%)
    all_to_all x1, blocking collectives, shards(): lax.all_to_all(parts, 'snap', split_axis=0, concat_axis=0)  63.8 us
    all_to_all x1, blocking collectives, shards(): lax.all_to_all(summed, 'snap', split_axis=0, concat_axis=0, axis_index_gr...  14.5 us
    pallas_call x6, Pallas kernels, call(): pl.pallas_call(kernel, in_specs=specs, out_specs=[anywhere if k in out_ap...  11.8 us
    ppermute x2, starting transfers between devices, shifted(): lax.ppermute(value, axis, [(i, (i + distance) % count) for i in range(cou...  5.83 us
    all_to_all x1, starting transfers between devices, shards(): packed = lax.all_to_all(packed, 'space', split_axis=0, concat_axis=0)  5.12 us
    unnamed x12, local copies, waits for them, and re-layouts  4.39 us
    ppermute x2, waiting for transfers between devices, flipped(): lax.ppermute(value, AXES, [(i, i ^ mask) for i in range(lax.axis_size(AXE...  3.68 us
    ppermute x2, waiting for transfers between devices, shifted(): lax.ppermute(value, axis, [(i, (i + distance) % count) for i in range(cou...  3.22 us
  transfers between devices with their start and end apart: 5, of which 4 were waited for; matrix products, arithmetic and copies ran while one was open for 0% of the time, Pallas kernels for 3%

profile of v2, /device:TPU:2, one launch (start us, length us, event | category | flops | bytes accessed | tf_op | source)
XLA Modules:
  0.0 119.4 jit_solution(5322896150417024657)
XLA Ops:
  0.6 0.8 fusion
  1.4 5.8 %collective-permute-start.1 = (bf16[32,512]{1,0:T(8,128)(2,1)S(1)}, bf16[32,512]{1,0:T(8,128)(2,1)S(1)}, u32[]{:S(2)}, u32[]{:S(2)}) collective-permute-start(bf16[32,512]{1,0:T(8,128)(2,1)S(1)} %get-tuple-element.19), channel_id=1, source_target_pairs={{0,240},{16,0},{32,16},{48,32},{64,48},{80,64},{96,80},{112,96},{1... | collective-permute-start | bytes 98312 | tf_op jit(solution)/shard_map/ppermute | solution.py:174
  7.2 0.0 collective-permute-start
  7.2 2.2 %copy-done = bf16[65536,32]{0,1:T(8,128)(2,1)S(1)} copy-done((bf16[65536,32]{0,1:T(8,128)(2,1)S(1)}, bf16[65536,32]{0,1:T(8,128)(2,1)}, u32[]{:S(2)}) %copy-start) | copy-done | bytes 4194328
  9.4 0.6 chunks.1.parts_in_ref
  10.0 0.0 collective-permute-done.1.after_ref
  10.0 3.2 %collective-permute-done.before_ref = bf16[32,512]{1,0:T(8,128)(2,1)S(1)} collective-permute-done((bf16[32,512]{1,0:T(8,128)(2,1)S(1)}, bf16[32,512]{1,0:T(8,128)(2,1)S(1)}, u32[]{:S(2)}, u32[]{:S(2)}) %collective-permute-start) | collective-permute-done | bytes 32800 | tf_op jit(solution)/shard_map/ppermute | solution.py:174
  13.3 0.0 copy-start.3
  13.3 0.0 copy-start.5
  13.3 63.8 %all_to_all.15 = bf16[16,32,4608]{2,1,0:T(8,128)(2,1)S(1)} all-to-all(bf16[16,32,4608]{2,1,0:T(8,128)(2,1)S(1)} %ends.1), channel_id=1, replica_groups=mesh['space'=16,'snap'=16] {'snap'}, dimensions={0} | all-to-all | bytes 9437184 | tf_op jit(solution)/shard_map/all_to_all | solution.py:228
  77.1 7.5 %inner.1 = (bf16[4096,512]{1,0:T(8,128)(2,1)}, f32[512,512]{1,0:T(8,128)S(1)}, bf16[512,4096]{1,0:T(8,128)(2,1)S(1)}, bf16[512,512]{1,0:T(8,128)(2,1)S(1)}, bf16[512,512]{1,0:T(8,128)(2,1)S(1)}) custom-call(s32[3,32]{1,0:T(4,128)S(1)} %bitcast.6, bf16[512,4608]{1,0:T(8,128)(2,1)S(1)} %bitcast.3, bf16[32,3,128,128]{3,2,1,0:T(8,128)(2,1)S(1)} %copy-done.3), custom_call_target="tpu_custom_call" | custom-call | flops 3288334336 | bytes 14680064 | tf_op jit(solution)/shard_map/inner/pallas_call | solution.py:180
  84.6 0.1 collective-permute-start.2
  84.7 1.9 %collective-permute-done.2.near_ref = bf16[512,512]{1,0:T(8,128)(2,1)S(1)} collective-permute-done((bf16[512,512]{1,0:T(8,128)(2,1)S(1)}, bf16[512,512]{1,0:T(8,128)(2,1)S(1)}, u32[]{:S(2)}, u32[]{:S(2)}) %collective-permute-start.2) | collective-permute-done | bytes 524320 | tf_op jit(solution)/shard_map/ppermute | solution.py:169
  86.6 2.3 %edge.1 = (bf16[4096,512]{1,0:T(8,128)(2,1)}, f32[8,32,512]{2,1,0:T(8,128)S(1)}, f32[8,32,512]{2,1,0:T(8,128)S(1)}) custom-call(s32[3,32]{1,0:T(4,128)S(1)} %bitcast.7, bf16[512,512]{1,0:T(8,128)(2,1)S(1)} %get-tuple-element.11.edge_ref, bf16[512,512]{1,0:T(8,128)(2,1)S(1)} %get-tuple-element.12.next_ref, ...), custom_call_target="tpu_custom_call", output_to_operand_aliasing={{0}: (6, {})} | custom-call | flops 469762048 | bytes 6291456 | tf_op jit(solution)/shard_map/edge/pallas_call | solution.py:180
  88.9 0.2 collective-permute-start.3
  89.1 1.8 %collective-permute-done.3 = f32[8,32,512]{2,1,0:T(8,128)S(1)} collective-permute-done((f32[8,32,512]{2,1,0:T(8,128)S(1)}, f32[8,32,512]{2,1,0:T(8,128)S(1)}, u32[]{:S(2)}, u32[]{:S(2)}) %collective-permute-start.3) | collective-permute-done | bytes 524320 | tf_op jit(solution)/shard_map/ppermute | solution.py:169
  90.9 0.1 add.3
  91.0 14.5 %all_to_all.16.parts_ref = f32[8,32,512]{2,1,0:T(8,128)S(1)} all-to-all(f32[8,32,512]{2,1,0:T(8,128)S(1)} %add.3), channel_id=1, replica_groups={{0,2,4,6,8,10,12,14},{1,3,5,7,9,11,13,15},{16,18,20,22,24,26,28,30},{17..., dimensions={0} | all-to-all | bytes 1048576 | tf_op jit(solution)/shard_map/all_to_all | solution.py:275
  105.4 0.8 pack.1
  106.2 5.1 %all-to-all-start.2 = ((f32[16,8,128]{2,1,0:T(8,128)}), f32[16,8,128]{2,1,0:T(8,128)S(1)}, u32[]{:S(2)}, u32[]{:S(2)}) async-start(f32[16,8,128]{2,1,0:T(8,128)} %pack.1), calls=%async_computation.2 | async-start | bytes 131072 | tf_op jit(solution)/shard_map/all_to_all | solution.py:278
  111.3 2.2 %copy-done.2 = bf16[512,4096]{1,0:T(8,128)(2,1)S(1)} copy-done((bf16[512,4096]{1,0:T(8,128)(2,1)S(1)}, bf16[512,4096]{1,0:T(8,128)(2,1)}, u32[]{:S(2)}) %copy-start.2) | copy-done | bytes 4194328
  113.5 2.8 %modes.1 = bf16[4096,128]{1,0:T(8,128)(2,1)} custom-call(bf16[512,4096]{1,0:T(8,128)(2,1)S(1)} %copy-done.2, bf16[512,128]{1,0:T(8,128)(2,1)S(1)} %copy-done.4), custom_call_target="tpu_custom_call" | custom-call | flops 536870912 | bytes 5242880 | tf_op jit(solution)/shard_map/modes/pallas_call | solution.py:242
  116.4 2.3 %all-to-all-done.2.packed_ref = f32[16,8,128]{2,1,0:T(8,128)S(1)} async-done(((f32[16,8,128]{2,1,0:T(8,128)}), f32[16,8,128]{2,1,0:T(8,128)S(1)}, u32[]{:S(2)}, u32[]{:S(2)}) %all-to-all-start.2) | async-done | bytes 65568 | tf_op jit(solution)/shard_map/all_to_all | solution.py:278
  118.7 0.7 unpack.1
  (9 shorter events, 0.0 us)
Async XLA Ops:
  1.4 8.6 %collective-permute-start.1 = (bf16[32,512]{1,0:T(8,128)(2,1)S(1)}, bf16[32,512]{1,0:T(8,128)(2,1)S(1)}, u32[]{:S(2)}, u32[]{:S(2)}) collective-permute-start(bf16[32,512]{1,0:T(8,128)(2,1)S(1)} %get-tuple-element.19), channel_id=1, source_target_pairs={{0,240},{16,0},{32,16},{48,32},{64,48},{80,64},{96,80},{112,96},{1... | collective-permute-start | bytes 98312 | tf_op jit(solution)/shard_map/ppermute | solution.py:174
  7.2 6.0 %collective-permute-start = (bf16[32,512]{1,0:T(8,128)(2,1)S(1)}, bf16[32,512]{1,0:T(8,128)(2,1)S(1)}, u32[]{:S(2)}, u32[]{:S(2)}) collective-permute-start(bf16[32,512]{1,0:T(8,128)(2,1)S(1)} %get-tuple-element.20), channel_id=1, source_target_pairs={{0,16},{16,32},{32,48},{48,64},{64,80},{80,96},{96,112},{112,128},... | collective-permute-start | bytes 98312 | tf_op jit(solution)/shard_map/ppermute | solution.py:174
  7.2 2.2 %copy-start = (bf16[65536,32]{0,1:T(8,128)(2,1)S(1)}, bf16[65536,32]{0,1:T(8,128)(2,1)}, u32[]{:S(2)}) copy-start(bf16[65536,32]{0,1:T(8,128)(2,1)} %param.4) | copy-start | bytes 12582916
  13.3 63.8 %copy-start.3 = (bf16[32,3,128,128]{3,2,1,0:T(8,128)(2,1)S(1)}, bf16[32,3,128,128]{3,2,1,0:T(8,128)(2,1)}, u32[]{:S(2)}) copy-start(bf16[32,3,128,128]{3,2,1,0:T(8,128)(2,1)} %mass_ref.3) | copy-start | bytes 9437188
  13.3 63.8 %copy-start.5 = (s32[32,3]{0,1:T(4,128)S(1)}, s32[32,3]{0,1:T(4,128)}, u32[]{:S(2)}) copy-start(s32[32,3]{0,1:T(4,128)} %param.6) | copy-start | bytes 1156
  84.6 4.3 %copy-start.1 = (bf16[512,4096]{1,0:T(8,128)(2,1)}, bf16[512,4096]{1,0:T(8,128)(2,1)S(1)}, u32[]{:S(2)}) copy-start(bf16[512,4096]{1,0:T(8,128)(2,1)S(1)} %get-tuple-element.18.field_ref) | copy-start | bytes 12582916
  84.6 2.0 %collective-permute-start.2 = (bf16[512,512]{1,0:T(8,128)(2,1)S(1)}, bf16[512,512]{1,0:T(8,128)(2,1)S(1)}, u32[]{:S(2)}, u32[]{:S(2)}) collective-permute-start(bf16[512,512]{1,0:T(8,128)(2,1)S(1)} %get-tuple-element.11.edge_ref), channel_id=1, source_target_pairs={{0,1},{1,0},{2,3},{3,2},{4,5},{5,4},{6,7},{7,6},{8,9},{9,8},{10,11... | collective-permute-start | bytes 1572872 | tf_op jit(solution)/shard_map/ppermute | solution.py:169
  86.6 24.7 %copy-start.4 = (bf16[512,128]{1,0:T(8,128)(2,1)S(1)}, bf16[512,128]{1,0:T(8,128)(2,1)}, u32[]{:S(2)}) copy-start(bf16[512,128]{1,0:T(8,128)(2,1)} %vectors_ref.1) | copy-start | bytes 393220
  88.9 2.0 %collective-permute-start.3 = (f32[8,32,512]{2,1,0:T(8,128)S(1)}, f32[8,32,512]{2,1,0:T(8,128)S(1)}, u32[]{:S(2)}, u32[]{:S(2)}) collective-permute-start(f32[8,32,512]{2,1,0:T(8,128)S(1)} %get-tuple-element.17), channel_id=1, source_target_pairs={{0,1},{1,0},{2,3},{3,2},{4,5},{5,4},{6,7},{7,6},{8,9},{9,8},{10,11... | collective-permute-start | bytes 1572872 | tf_op jit(solution)/shard_map/ppermute | solution.py:169
  106.2 12.5 %all-to-all-start.2 = ((f32[16,8,128]{2,1,0:T(8,128)}), f32[16,8,128]{2,1,0:T(8,128)S(1)}, u32[]{:S(2)}, u32[]{:S(2)}) async-start(f32[16,8,128]{2,1,0:T(8,128)} %pack.1), calls=%async_computation.2 | async-start | bytes 131072 | tf_op jit(solution)/shard_map/all_to_all | solution.py:278
  111.3 2.2 %copy-start.2 = (bf16[512,4096]{1,0:T(8,128)(2,1)S(1)}, bf16[512,4096]{1,0:T(8,128)(2,1)}, u32[]{:S(2)}) copy-start(bf16[512,4096]{1,0:T(8,128)(2,1)} %copy-done.1) | copy-start | bytes 12582916

commit v3 on v2

--- a/solution.py
+++ b/solution.py
@@ -20,8 +20,7 @@
 def weigh(place, blocks, mass_ref, field_ref, weighted_ref, size):
     for k in range(blocks):
         near = [field_ref[:, pl.ds(pl.multiple_of(place(k, j) * size, size), size)] for j in range(3)]
-        mass = [mass_ref[k, j] for j in range(3)]
-        block = contract(jnp.concatenate(mass, axis=1), jnp.concatenate(near, axis=1), 1, 1)
+        block = sum(contract(mass_ref[k, j], near[j], 1, 1) for j in range(3))
         weighted_ref[k * size : (k + 1) * size, :] = block.astype(weighted_ref.dtype)
 
 
@@ -62,7 +61,14 @@
         copy.wait()
 
 
-def inner_kernel(neighbours_ref, field_ref, mass_ref, weighted_ref, corr_ref, copy_ref, edge_ref, next_ref, block,
+def cut_kernel(field_ref, mass_ref, edge_ref):
+    del mass_ref
+    width = edge_ref.shape[1]
+    core = here()[1]
+    edge_ref[...] = field_ref[:, pl.ds(pl.multiple_of((1 - core) * (field_ref.shape[1] - width), width), width)]
+
+
+def inner_kernel(neighbours_ref, field_ref, mass_ref, weighted_ref, corr_ref, copy_ref, next_ref, block,
                  block_sems, copy_sem):
     count, _, size, _ = mass_ref.shape
     width = STEP * size
@@ -72,7 +78,6 @@
     own = pl.ds(pl.multiple_of((1 - core) * width, width), count * size)
     copy = pltpu.make_async_copy(field_ref.at[:, own], copy_ref, copy_sem)
     copy.start()
-    edge_ref[...] = field_ref[:, pl.ds(pl.multiple_of((1 - core) * groups * width, width), width)]
     next_ref[...] = field_ref[:, pl.ds(pl.multiple_of(core * width + (1 - core) * (groups - 1) * width, width), width)]
     writes = []
     for step in range(groups - 1):
@@ -228,17 +233,18 @@
     field = lax.all_to_all(parts, "snap", split_axis=0, concat_axis=0).reshape(snaps, rows + width)
     listed = neighbours.T
     per_row = 2 * snaps * (3 * size + snaps)
-    weighted, corr, field, edge, following = call(
+    (edge,) = call(cut_kernel, "cut", (field, mass_blocks), [half(snaps, width)], MIB)
+    near = flipped(edge, 1)
+    weighted, corr, field, following = call(
         inner_kernel,
         "inner",
         (listed, field, mass_blocks),
-        [half(rows, snaps), single(snaps, snaps), half(snaps, rows)] + [half(snaps, width)] * 2,
+        [half(rows, snaps), single(snaps, snaps), half(snaps, rows)] + [half(snaps, width)],
         14 * MIB,
         (rows - width) * per_row,
         out_apart=(0, 2),
         scratch=[pltpu.VMEM((2, width, snaps), jnp.bfloat16), sems((2,)), sems(())],
     )
-    near = flipped(edge, 1)
     modes = pl.pallas_call(
         modes_kernel,
         grid=(rows // 1024,),

time: 120 us -> 118 us (0.983)
  waiting for transfers between devices: 9.21 us -> 7.43 us
    ppermute x2, waiting for transfers between devices: 3.68 us -> 1.9 us  [flipped(): lax.ppermute(value, AXES, [(i, i ^ mask) for i in range(lax.axis_size(AXE...]
    pallas_call x6 -> x7, Pallas kernels: 11.8 us -> 11.5 us  [call(): pl.pallas_call(kernel, in_specs=specs, out_specs=[anywhere if k in out_ap...]
  transfers between devices with their start and end apart: 5 -> 5, of which waited for: 4 -> 3; matrix products, arithmetic and copies ran while one was open for 0% -> 0% of each run, Pallas kernels for 3% -> 9%
where the time goes in v3:
time: 118 us
  blocking collectives  78.3 us (66%)
  Pallas kernels  14.4 us (12%)
  starting transfers between devices  11.1 us (9%)
  waiting for transfers between devices  7.43 us (6%)
  local copies, waits for them, and re-layouts  5.71 us (5%)
    all_to_all x1, blocking collectives, shards(): lax.all_to_all(parts, 'snap', split_axis=0, concat_axis=0)  63.8 us
    all_to_all x1, blocking collectives, shards(): lax.all_to_all(summed, 'snap', split_axis=0, concat_axis=0, axis_index_gr...  14.5 us
    pallas_call x7, Pallas kernels, call(): pl.pallas_call(kernel, in_specs=specs, out_specs=[anywhere if k in out_ap...  11.5 us
    ppermute x2, starting transfers between devices, shifted(): lax.ppermute(value, axis, [(i, (i + distance) % count) for i in range(cou...  5.83 us
    all_to_all x1, starting transfers between devices, shards(): packed = lax.all_to_all(packed, 'space', split_axis=0, concat_axis=0)  5.11 us
    unnamed x12, local copies, waits for them, and re-layouts  4.93 us
    ppermute x2, waiting for transfers between devices, shifted(): lax.ppermute(value, axis, [(i, (i + distance) % count) for i in range(cou...  3.22 us
    pallas_call x1, Pallas kernels, shards(): pl.pallas_call(modes_kernel, grid=(rows // 1024,), in_specs=[pl.BlockSpec...  2.84 us
  transfers between devices with their start and end apart: 5, of which 3 were waited for; matrix products, arithmetic and copies ran while one was open for 0% of the time, Pallas kernels for 9%

profile of v3, /device:TPU:2, one launch (start us, length us, event | category | flops | bytes accessed | tf_op | source)
XLA Modules:
  0.0 117.7 jit_solution(11196971188363525037)
XLA Ops:
  0.6 0.8 fusion
  1.4 5.8 %collective-permute-start.1 = (bf16[32,512]{1,0:T(8,128)(2,1)S(1)}, bf16[32,512]{1,0:T(8,128)(2,1)S(1)}, u32[]{:S(2)}, u32[]{:S(2)}) collective-permute-start(bf16[32,512]{1,0:T(8,128)(2,1)S(1)} %get-tuple-element.17), channel_id=1, source_target_pairs={{0,240},{16,0},{32,16},{48,32},{64,48},{80,64},{96,80},{112,96},{1... | collective-permute-start | bytes 98312 | tf_op jit(solution)/shard_map/ppermute | solution.py:179
  7.2 0.0 collective-permute-start
  7.2 2.2 %copy-done.1 = bf16[65536,32]{0,1:T(8,128)(2,1)S(1)} copy-done((bf16[65536,32]{0,1:T(8,128)(2,1)S(1)}, bf16[65536,32]{0,1:T(8,128)(2,1)}, u32[]{:S(2)}) %copy-start.1) | copy-done | bytes 4194328
  9.4 0.6 chunks.1.parts_in_ref
  10.0 0.0 collective-permute-done.1.after_ref
  10.0 3.2 %collective-permute-done.before_ref = bf16[32,512]{1,0:T(8,128)(2,1)S(1)} collective-permute-done((bf16[32,512]{1,0:T(8,128)(2,1)S(1)}, bf16[32,512]{1,0:T(8,128)(2,1)S(1)}, u32[]{:S(2)}, u32[]{:S(2)}) %collective-permute-start) | collective-permute-done | bytes 32800 | tf_op jit(solution)/shard_map/ppermute | solution.py:179
  13.3 0.0 copy-start
  13.3 63.8 %all_to_all.15 = bf16[16,32,4608]{2,1,0:T(8,128)(2,1)S(1)} all-to-all(bf16[16,32,4608]{2,1,0:T(8,128)(2,1)S(1)} %ends.1), channel_id=1, replica_groups=mesh['space'=16,'snap'=16] {'snap'}, dimensions={0} | all-to-all | bytes 9437184 | tf_op jit(solution)/shard_map/all_to_all | solution.py:233
  77.2 0.1 collective-permute-start.2
  77.3 0.5 copy-done.5
  77.8 7.2 %inner.1 = (bf16[4096,512]{1,0:T(8,128)(2,1)}, f32[512,512]{1,0:T(8,128)S(1)}, bf16[512,4096]{1,0:T(8,128)(2,1)S(1)}, bf16[512,512]{1,0:T(8,128)(2,1)S(1)}) custom-call(s32[3,32]{1,0:T(4,128)S(1)} %bitcast.7, bf16[512,4608]{1,0:T(8,128)(2,1)S(1)} %bitcast.4, bf16[32,3,128,128]{3,2,1,0:T(8,128)(2,1)S(1)} %copy-done), custom_call_target="tpu_custom_call" | custom-call | flops 3288334336 | bytes 14680064 | tf_op jit(solution)/shard_map/inner/pallas_call | solution.py:185
  85.0 0.0 copy-start.4
  85.0 2.2 %edge.1 = (bf16[4096,512]{1,0:T(8,128)(2,1)}, f32[8,32,512]{2,1,0:T(8,128)S(1)}, f32[8,32,512]{2,1,0:T(8,128)S(1)}) custom-call(s32[3,32]{1,0:T(4,128)S(1)} %bitcast.8, bf16[512,512]{1,0:T(8,128)(2,1)S(1)} %cut.1.edge_ref, bf16[512,512]{1,0:T(8,128)(2,1)S(1)} %get-tuple-element.10.next_ref, ...), custom_call_target="tpu_custom_call", output_to_operand_aliasing={{0}: (6, {})} | custom-call | flops 469762048 | bytes 6291456 | tf_op jit(solution)/shard_map/edge/pallas_call | solution.py:185
  87.3 0.1 collective-permute-start.3
  87.4 1.9 %collective-permute-done.3 = f32[8,32,512]{2,1,0:T(8,128)S(1)} collective-permute-done((f32[8,32,512]{2,1,0:T(8,128)S(1)}, f32[8,32,512]{2,1,0:T(8,128)S(1)}, u32[]{:S(2)}, u32[]{:S(2)}) %collective-permute-start.3) | collective-permute-done | bytes 524320 | tf_op jit(solution)/shard_map/ppermute | solution.py:174
  89.3 0.1 add.3
  89.4 14.5 %all_to_all.16.parts_ref = f32[8,32,512]{2,1,0:T(8,128)S(1)} all-to-all(f32[8,32,512]{2,1,0:T(8,128)S(1)} %add.3), channel_id=1, replica_groups={{0,2,4,6,8,10,12,14},{1,3,5,7,9,11,13,15},{16,18,20,22,24,26,28,30},{17..., dimensions={0} | all-to-all | bytes 1048576 | tf_op jit(solution)/shard_map/all_to_all | solution.py:281
  103.8 0.8 pack.1
  104.6 5.1 %all-to-all-start.2 = ((f32[16,8,128]{2,1,0:T(8,128)}), f32[16,8,128]{2,1,0:T(8,128)S(1)}, u32[]{:S(2)}, u32[]{:S(2)}) async-start(f32[16,8,128]{2,1,0:T(8,128)} %pack.1), calls=%async_computation.2 | async-start | bytes 131072 | tf_op jit(solution)/shard_map/all_to_all | solution.py:284
  109.7 2.2 %copy-done.3 = bf16[512,4096]{1,0:T(8,128)(2,1)S(1)} copy-done((bf16[512,4096]{1,0:T(8,128)(2,1)S(1)}, bf16[512,4096]{1,0:T(8,128)(2,1)}, u32[]{:S(2)}) %copy-start.3) | copy-done | bytes 4194328
  111.9 2.8 %modes.1 = bf16[4096,128]{1,0:T(8,128)(2,1)} custom-call(bf16[512,4096]{1,0:T(8,128)(2,1)S(1)} %copy-done.3, bf16[512,128]{1,0:T(8,128)(2,1)S(1)} %copy-done.4), custom_call_target="tpu_custom_call" | custom-call | flops 536870912 | bytes 5242880 | tf_op jit(solution)/shard_map/modes/pallas_call | solution.py:248
  114.7 2.3 %all-to-all-done.2.packed_ref = f32[16,8,128]{2,1,0:T(8,128)S(1)} async-done(((f32[16,8,128]{2,1,0:T(8,128)}), f32[16,8,128]{2,1,0:T(8,128)S(1)}, u32[]{:S(2)}, u32[]{:S(2)}) %all-to-all-start.2) | async-done | bytes 65568 | tf_op jit(solution)/shard_map/all_to_all | solution.py:284
  117.0 0.7 unpack.1
  (10 shorter events, 0.1 us)
Async XLA Ops:
  1.4 8.6 %collective-permute-start.1 = (bf16[32,512]{1,0:T(8,128)(2,1)S(1)}, bf16[32,512]{1,0:T(8,128)(2,1)S(1)}, u32[]{:S(2)}, u32[]{:S(2)}) collective-permute-start(bf16[32,512]{1,0:T(8,128)(2,1)S(1)} %get-tuple-element.17), channel_id=1, source_target_pairs={{0,240},{16,0},{32,16},{48,32},{64,48},{80,64},{96,80},{112,96},{1... | collective-permute-start | bytes 98312 | tf_op jit(solution)/shard_map/ppermute | solution.py:179
  7.2 6.0 %collective-permute-start = (bf16[32,512]{1,0:T(8,128)(2,1)S(1)}, bf16[32,512]{1,0:T(8,128)(2,1)S(1)}, u32[]{:S(2)}, u32[]{:S(2)}) collective-permute-start(bf16[32,512]{1,0:T(8,128)(2,1)S(1)} %get-tuple-element.18), channel_id=1, source_target_pairs={{0,16},{16,32},{32,48},{48,64},{64,80},{80,96},{96,112},{112,128},... | collective-permute-start | bytes 98312 | tf_op jit(solution)/shard_map/ppermute | solution.py:179
  7.2 2.2 %copy-start.1 = (bf16[65536,32]{0,1:T(8,128)(2,1)S(1)}, bf16[65536,32]{0,1:T(8,128)(2,1)}, u32[]{:S(2)}) copy-start(bf16[65536,32]{0,1:T(8,128)(2,1)} %param.4) | copy-start | bytes 12582916
  13.3 63.8 %copy-start = (bf16[32,3,128,128]{3,2,1,0:T(8,128)(2,1)S(1)}, bf16[32,3,128,128]{3,2,1,0:T(8,128)(2,1)}, u32[]{:S(2)}) copy-start(bf16[32,3,128,128]{3,2,1,0:T(8,128)(2,1)} %mass_ref.5) | copy-start | bytes 9437188
  77.1 0.7 copy-start.5
  77.2 7.9 %collective-permute-start.2 = (bf16[512,512]{1,0:T(8,128)(2,1)S(1)}, bf16[512,512]{1,0:T(8,128)(2,1)S(1)}, u32[]{:S(2)}, u32[]{:S(2)}) collective-permute-start(bf16[512,512]{1,0:T(8,128)(2,1)S(1)} %cut.1.edge_ref), channel_id=1, source_target_pairs={{0,1},{1,0},{2,3},{3,2},{4,5},{5,4},{6,7},{7,6},{8,9},{9,8},{10,11... | collective-permute-start | bytes 1572872 | tf_op jit(solution)/shard_map/ppermute | solution.py:174
  85.0 2.3 %copy-start.2 = (bf16[512,4096]{1,0:T(8,128)(2,1)}, bf16[512,4096]{1,0:T(8,128)(2,1)S(1)}, u32[]{:S(2)}) copy-start(bf16[512,4096]{1,0:T(8,128)(2,1)S(1)} %get-tuple-element.16.field_ref) | copy-start | bytes 12582916
  85.0 24.7 %copy-start.4 = (bf16[512,128]{1,0:T(8,128)(2,1)S(1)}, bf16[512,128]{1,0:T(8,128)(2,1)}, u32[]{:S(2)}) copy-start(bf16[512,128]{1,0:T(8,128)(2,1)} %vectors_ref.1) | copy-start | bytes 393220
  87.3 2.0 %collective-permute-start.3 = (f32[8,32,512]{2,1,0:T(8,128)S(1)}, f32[8,32,512]{2,1,0:T(8,128)S(1)}, u32[]{:S(2)}, u32[]{:S(2)}) collective-permute-start(f32[8,32,512]{2,1,0:T(8,128)S(1)} %get-tuple-element.15), channel_id=1, source_target_pairs={{0,1},{1,0},{2,3},{3,2},{4,5},{5,4},{6,7},{7,6},{8,9},{9,8},{10,11... | collective-permute-start | bytes 1572872 | tf_op jit(solution)/shard_map/ppermute | solution.py:174
  104.6 12.5 %all-to-all-start.2 = ((f32[16,8,128]{2,1,0:T(8,128)}), f32[16,8,128]{2,1,0:T(8,128)S(1)}, u32[]{:S(2)}, u32[]{:S(2)}) async-start(f32[16,8,128]{2,1,0:T(8,128)} %pack.1), calls=%async_computation.2 | async-start | bytes 131072 | tf_op jit(solution)/shard_map/all_to_all | solution.py:284
  109.7 2.2 %copy-start.3 = (bf16[512,4096]{1,0:T(8,128)(2,1)S(1)}, bf16[512,4096]{1,0:T(8,128)(2,1)}, u32[]{:S(2)}) copy-start(bf16[512,4096]{1,0:T(8,128)(2,1)} %copy-done.2) | copy-start | bytes 12582916

commit v4 on v3

--- a/solution.py
+++ b/solution.py
@@ -29,11 +29,13 @@
     return lax.axis_index("space") * lax.axis_size("snap") + snap, lax.rem(snap, 2)
 
 
-def chunks_kernel(field_ref, parts_ref, sems):
+def chunks_kernel(field_ref, parts_ref, first_ref, sems):
     group, _, length = parts_ref.shape
     own = field_ref.shape[1] // group
     halo = length - own
     copies = []
+    copies.append(pltpu.make_async_copy(field_ref.at[:, pl.ds(0, halo)], first_ref, sems.at[group]))
+    copies[-1].start()
     for k in range(group):
         start, to, size = k * own - (1 - k % 2) * halo, 0, length
         if k == 0:
@@ -214,11 +216,18 @@
     sems = pltpu.SemaphoreType.DMA
     flat = snapshots.T
     before = shifted(flat[:, cells - width :], "space", 1)
-    after = shifted(flat[:, :width], "space", -1)
     chunked = [half(group, mine, rows + width)]
-    (parts,) = call(
-        chunks_kernel, "chunks", (flat,), chunked, 8 * MIB, apart=(0,), out_apart=(0,), scratch=[sems((group,))]
-    )
+    parts, first = call(
+        chunks_kernel,
+        "chunks",
+        (flat,),
+        chunked + [half(mine, width)],
+        8 * MIB,
+        apart=(0,),
+        out_apart=(0, 1),
+        scratch=[sems((group + 1,))],
+    )
+    after = shifted(first, "space", -1)
     (parts,) = call(
         ends_kernel,
         "ends",

time: 118 us -> 119 us (level)
  starting transfers between devices: 11.1 us -> 14 us
  waiting for transfers between devices: 7.43 us -> 5.71 us
    all_to_all x1, starting transfers between devices: 5.11 us -> 7.91 us  [shards(): packed = lax.all_to_all(packed, 'space', split_axis=0, concat_axis=0)]
    ppermute x2, waiting for transfers between devices: 3.22 us -> 1.6 us  [shifted(): lax.ppermute(value, axis, [(i, (i + distance) % count) for i in range(cou...]
where the time goes in v4:
time: 119 us
  blocking collectives  78.3 us (66%)
  Pallas kernels  14.3 us (12%)
  starting transfers between devices  14 us (12%)
  waiting for transfers between devices  5.71 us (5%)
  local copies, waits for them, and re-layouts  5.69 us (5%)
    all_to_all x1, blocking collectives, shards(): lax.all_to_all(parts, 'snap', split_axis=0, concat_axis=0)  63.8 us
    all_to_all x1, blocking collectives, shards(): lax.all_to_all(summed, 'snap', split_axis=0, concat_axis=0, axis_index_gr...  14.5 us
    pallas_call x7, Pallas kernels, call(): pl.pallas_call(kernel, in_specs=specs, out_specs=[anywhere if k in out_ap...  11.4 us
    all_to_all x1, starting transfers between devices, shards(): packed = lax.all_to_all(packed, 'space', split_axis=0, concat_axis=0)  7.91 us
    ppermute x2, starting transfers between devices, shifted(): lax.ppermute(value, axis, [(i, (i + distance) % count) for i in range(cou...  5.91 us
    unnamed x12, local copies, waits for them, and re-layouts  4.93 us
    pallas_call x1, Pallas kernels, shards(): pl.pallas_call(modes_kernel, grid=(rows // 1024,), in_specs=[pl.BlockSpec...  2.84 us
  transfers between devices with their start and end apart: 5, of which 3 were waited for; matrix products, arithmetic and copies ran while one was open for 0% of the time, Pallas kernels for 9%

profile of v4, /device:TPU:2, one launch (start us, length us, event | category | flops | bytes accessed | tf_op | source)
XLA Modules:
  0.0 118.8 jit_solution(7979908910238222439)
XLA Ops:
  0.6 0.8 slice.4
  1.4 1.9 %collective-permute-start = (bf16[32,512]{1,0:T(8,128)(2,1)S(1)}, bf16[32,512]{1,0:T(8,128)(2,1)S(1)}, u32[]{:S(2)}, u32[]{:S(2)}) collective-permute-start(bf16[32,512]{1,0:T(8,128)(2,1)S(1)} %slice.4), channel_id=1, source_target_pairs={{0,16},{16,32},{32,48},{48,64},{64,80},{80,96},{96,112},{112,128},... | collective-permute-start | bytes 98312 | tf_op jit(solution)/shard_map/ppermute | solution.py:181
  3.3 2.2 %copy-done.1 = bf16[65536,32]{0,1:T(8,128)(2,1)S(1)} copy-done((bf16[65536,32]{0,1:T(8,128)(2,1)S(1)}, bf16[65536,32]{0,1:T(8,128)(2,1)}, u32[]{:S(2)}) %copy-start.1) | copy-done | bytes 4194328
  5.5 0.6 chunks.1
  6.1 4.0 %collective-permute-start.1 = (bf16[32,512]{1,0:T(8,128)(2,1)S(1)}, bf16[32,512]{1,0:T(8,128)(2,1)S(1)}, u32[]{:S(2)}, u32[]{:S(2)}) collective-permute-start(bf16[32,512]{1,0:T(8,128)(2,1)S(1)} %get-tuple-element.12), channel_id=1, source_target_pairs={{0,240},{16,0},{32,16},{48,32},{64,48},{80,64},{96,80},{112,96},{1... | collective-permute-start | bytes 98312 | tf_op jit(solution)/shard_map/ppermute | solution.py:181
  10.1 0.0 collective-permute-done.before_ref
  10.1 1.6 %collective-permute-done.1.after_ref = bf16[32,512]{1,0:T(8,128)(2,1)S(1)} collective-permute-done((bf16[32,512]{1,0:T(8,128)(2,1)S(1)}, bf16[32,512]{1,0:T(8,128)(2,1)S(1)}, u32[]{:S(2)}, u32[]{:S(2)}) %collective-permute-start.1) | collective-permute-done | bytes 32800 | tf_op jit(solution)/shard_map/ppermute | solution.py:181
  11.7 0.0 copy-start
  11.8 63.8 %all_to_all.15 = bf16[16,32,4608]{2,1,0:T(8,128)(2,1)S(1)} all-to-all(bf16[16,32,4608]{2,1,0:T(8,128)(2,1)S(1)} %ends.1), channel_id=1, replica_groups=mesh['space'=16,'snap'=16] {'snap'}, dimensions={0} | all-to-all | bytes 9437184 | tf_op jit(solution)/shard_map/all_to_all | solution.py:242
  75.6 0.1 collective-permute-start.2
  75.7 0.5 copy-done.5
  76.3 7.1 %inner.1 = (bf16[4096,512]{1,0:T(8,128)(2,1)}, f32[512,512]{1,0:T(8,128)S(1)}, bf16[512,4096]{1,0:T(8,128)(2,1)S(1)}, bf16[512,512]{1,0:T(8,128)(2,1)S(1)}) custom-call(s32[3,32]{1,0:T(4,128)S(1)} %bitcast.7, bf16[512,4608]{1,0:T(8,128)(2,1)S(1)} %bitcast.4, bf16[32,3,128,128]{3,2,1,0:T(8,128)(2,1)S(1)} %copy-done), custom_call_target="tpu_custom_call" | custom-call | flops 3288334336 | bytes 14680064 | tf_op jit(solution)/shard_map/inner/pallas_call | solution.py:187
  83.4 0.0 copy-start.4
  83.4 2.2 %edge.1 = (bf16[4096,512]{1,0:T(8,128)(2,1)}, f32[8,32,512]{2,1,0:T(8,128)S(1)}, f32[8,32,512]{2,1,0:T(8,128)S(1)}) custom-call(s32[3,32]{1,0:T(4,128)S(1)} %bitcast.8, bf16[512,512]{1,0:T(8,128)(2,1)S(1)} %cut.1.edge_ref, bf16[512,512]{1,0:T(8,128)(2,1)S(1)} %get-tuple-element.14.next_ref, ...), custom_call_target="tpu_custom_call", output_to_operand_aliasing={{0}: (6, {})} | custom-call | flops 469762048 | bytes 6291456 | tf_op jit(solution)/shard_map/edge/pallas_call | solution.py:187
  85.6 0.1 collective-permute-start.3
  85.7 1.9 %collective-permute-done.3 = f32[8,32,512]{2,1,0:T(8,128)S(1)} collective-permute-done((f32[8,32,512]{2,1,0:T(8,128)S(1)}, f32[8,32,512]{2,1,0:T(8,128)S(1)}, u32[]{:S(2)}, u32[]{:S(2)}) %collective-permute-start.3) | collective-permute-done | bytes 524320 | tf_op jit(solution)/shard_map/ppermute | solution.py:176
  87.6 0.1 add.3
  87.7 14.5 %all_to_all.16.parts_ref = f32[8,32,512]{2,1,0:T(8,128)S(1)} all-to-all(f32[8,32,512]{2,1,0:T(8,128)S(1)} %add.3), channel_id=1, replica_groups={{0,2,4,6,8,10,12,14},{1,3,5,7,9,11,13,15},{16,18,20,22,24,26,28,30},{17..., dimensions={0} | all-to-all | bytes 1048576 | tf_op jit(solution)/shard_map/all_to_all | solution.py:290
  102.2 0.8 pack.1
  102.9 7.9 %all-to-all-start.2 = ((f32[16,8,128]{2,1,0:T(8,128)}), f32[16,8,128]{2,1,0:T(8,128)S(1)}, u32[]{:S(2)}, u32[]{:S(2)}) async-start(f32[16,8,128]{2,1,0:T(8,128)} %pack.1), calls=%async_computation.2 | async-start | bytes 131072 | tf_op jit(solution)/shard_map/all_to_all | solution.py:293
  110.8 2.2 %copy-done.3 = bf16[512,4096]{1,0:T(8,128)(2,1)S(1)} copy-done((bf16[512,4096]{1,0:T(8,128)(2,1)S(1)}, bf16[512,4096]{1,0:T(8,128)(2,1)}, u32[]{:S(2)}) %copy-start.3) | copy-done | bytes 4194328
  113.0 2.8 %modes.1 = bf16[4096,128]{1,0:T(8,128)(2,1)} custom-call(bf16[512,4096]{1,0:T(8,128)(2,1)S(1)} %copy-done.3, bf16[512,128]{1,0:T(8,128)(2,1)S(1)} %copy-done.4), custom_call_target="tpu_custom_call" | custom-call | flops 536870912 | bytes 5242880 | tf_op jit(solution)/shard_map/modes/pallas_call | solution.py:257
  115.9 2.2 %all-to-all-done.2.packed_ref = f32[16,8,128]{2,1,0:T(8,128)S(1)} async-done(((f32[16,8,128]{2,1,0:T(8,128)}), f32[16,8,128]{2,1,0:T(8,128)S(1)}, u32[]{:S(2)}, u32[]{:S(2)}) %all-to-all-start.2) | async-done | bytes 65568 | tf_op jit(solution)/shard_map/all_to_all | solution.py:293
  118.1 0.7 unpack.1
  (10 shorter events, 0.1 us)
Async XLA Ops:
  1.4 8.7 %collective-permute-start = (bf16[32,512]{1,0:T(8,128)(2,1)S(1)}, bf16[32,512]{1,0:T(8,128)(2,1)S(1)}, u32[]{:S(2)}, u32[]{:S(2)}) collective-permute-start(bf16[32,512]{1,0:T(8,128)(2,1)S(1)} %slice.4), channel_id=1, source_target_pairs={{0,16},{16,32},{32,48},{48,64},{64,80},{80,96},{96,112},{112,128},... | collective-permute-start | bytes 98312 | tf_op jit(solution)/shard_map/ppermute | solution.py:181
  3.3 2.2 %copy-start.1 = (bf16[65536,32]{0,1:T(8,128)(2,1)S(1)}, bf16[65536,32]{0,1:T(8,128)(2,1)}, u32[]{:S(2)}) copy-start(bf16[65536,32]{0,1:T(8,128)(2,1)} %param.4) | copy-start | bytes 12582916
  6.1 5.6 %collective-permute-start.1 = (bf16[32,512]{1,0:T(8,128)(2,1)S(1)}, bf16[32,512]{1,0:T(8,128)(2,1)S(1)}, u32[]{:S(2)}, u32[]{:S(2)}) collective-permute-start(bf16[32,512]{1,0:T(8,128)(2,1)S(1)} %get-tuple-element.12), channel_id=1, source_target_pairs={{0,240},{16,0},{32,16},{48,32},{64,48},{80,64},{96,80},{112,96},{1... | collective-permute-start | bytes 98312 | tf_op jit(solution)/shard_map/ppermute | solution.py:181
  11.7 63.8 %copy-start = (bf16[32,3,128,128]{3,2,1,0:T(8,128)(2,1)S(1)}, bf16[32,3,128,128]{3,2,1,0:T(8,128)(2,1)}, u32[]{:S(2)}) copy-start(bf16[32,3,128,128]{3,2,1,0:T(8,128)(2,1)} %mass_ref.5) | copy-start | bytes 9437188
  75.6 0.7 copy-start.5
  75.6 7.7 %collective-permute-start.2 = (bf16[512,512]{1,0:T(8,128)(2,1)S(1)}, bf16[512,512]{1,0:T(8,128)(2,1)S(1)}, u32[]{:S(2)}, u32[]{:S(2)}) collective-permute-start(bf16[512,512]{1,0:T(8,128)(2,1)S(1)} %cut.1.edge_ref), channel_id=1, source_target_pairs={{0,1},{1,0},{2,3},{3,2},{4,5},{5,4},{6,7},{7,6},{8,9},{9,8},{10,11... | collective-permute-start | bytes 1572872 | tf_op jit(solution)/shard_map/ppermute | solution.py:176
  83.3 2.3 %copy-start.2 = (bf16[512,4096]{1,0:T(8,128)(2,1)}, bf16[512,4096]{1,0:T(8,128)(2,1)S(1)}, u32[]{:S(2)}) copy-start(bf16[512,4096]{1,0:T(8,128)(2,1)S(1)} %get-tuple-element.20.field_ref) | copy-start | bytes 12582916
  83.4 27.5 %copy-start.4 = (bf16[512,128]{1,0:T(8,128)(2,1)S(1)}, bf16[512,128]{1,0:T(8,128)(2,1)}, u32[]{:S(2)}) copy-start(bf16[512,128]{1,0:T(8,128)(2,1)} %vectors_ref.1) | copy-start | bytes 393220
  85.6 2.0 %collective-permute-start.3 = (f32[8,32,512]{2,1,0:T(8,128)S(1)}, f32[8,32,512]{2,1,0:T(8,128)S(1)}, u32[]{:S(2)}, u32[]{:S(2)}) collective-permute-start(f32[8,32,512]{2,1,0:T(8,128)S(1)} %get-tuple-element.19), channel_id=1, source_target_pairs={{0,1},{1,0},{2,3},{3,2},{4,5},{5,4},{6,7},{7,6},{8,9},{9,8},{10,11... | collective-permute-start | bytes 1572872 | tf_op jit(solution)/shard_map/ppermute | solution.py:176
  102.9 15.2 %all-to-all-start.2 = ((f32[16,8,128]{2,1,0:T(8,128)}), f32[16,8,128]{2,1,0:T(8,128)S(1)}, u32[]{:S(2)}, u32[]{:S(2)}) async-start(f32[16,8,128]{2,1,0:T(8,128)} %pack.1), calls=%async_computation.2 | async-start | bytes 131072 | tf_op jit(solution)/shard_map/all_to_all | solution.py:293
  110.8 2.2 %copy-start.3 = (bf16[512,4096]{1,0:T(8,128)(2,1)S(1)}, bf16[512,4096]{1,0:T(8,128)(2,1)}, u32[]{:S(2)}) copy-start(bf16[512,4096]{1,0:T(8,128)(2,1)} %copy-done.2) | copy-start | bytes 12582916
